TPU v7x, 32 devices: a whole 2x2x4 slice. The times are simulated.
32 devices in a mesh: clips: 2 (over x), lon: 16 (over z, y, core).
Axes of the slice: x: 2, y: 2, z: 4, core: 2. Of those that a mesh axis runs over, the one named last changes fastest.
Arguments:
- video_span: bfloat16 [2, 180, 128, 192], P(None, 'clips', 'lon'), parts along dimension 1, may hold values from -6 to 6
- caches: bfloat16 [3, 2, 180, 128, 192], P(None, None, 'clips', 'lon'), parts along dimension 2, may hold values from -0.25 to 1.5
- norm_gains: float32 [3, 192], replicated, may hold values from 0.5 to 1.5
- shifts: float32 [3, 192], replicated, may hold values from -0.5 to 0.5
- weights: bfloat16 [3, 5184, 192], replicated, may hold values from -0.078125 to 0.078125
- biases: float32 [3, 192], replicated, may hold values from -0.5 to 0.5
Outputs:
- encoded: bfloat16 [2, 180, 128, 192], P(None, 'clips', 'lon'), parts along dimension 1
- carried_frames: bfloat16 [3, 2, 180, 128, 192], P(None, None, 'clips', 'lon'), parts along dimension 2
There are 2 independent parts, one for each index of `clips`. A program takes and returns all parts, laid end to end along the dimension named above; an argument that names none is the same for every part. Nothing has to cross between parts.
All inputs are finite; a program needn't handle non-finite values.
Results may differ from a plain program's by a relative error of at most 0.0031.
Values may be sent and summed in bfloat16 or wider, within the bound.
A program may use at most 192 MiB of HBM per device.

v0:
```python
import functools

import jax
import jax.numpy as jnp
from jax import lax
from jax.experimental import pallas as pl
from jax.experimental.pallas import tpu as pltpu
from jax.sharding import PartitionSpec as P

GROUPS = 32
EPSILON = 1e-06
MESH = pl.DeviceIdType.MESH
LO = 128
F32 = jnp.float32
BF16 = jnp.bfloat16


def kernel(
    peers,
    video_hbm, caches_hbm, gains_ref, shifts_ref, weights_hbm, biases_ref,
    encoded_hbm, carried_hbm,
    video, caches, raw, weights, x, cx, acc, edge_out, edge_in, cedge_out, cedge_in,
    hx, chx, jc, ja, stat_out, stat_in, params, carried, encoded,
    in_sem, w_sem, out_sem, stat_send, stat_recv, edge_send, edge_recv, cedge_send, cedge_recv,
):
    frames, height, width, channels = video.shape
    layers = caches.shape[0]
    half = height // 2
    rows = half * 16
    total = frames * rows
    hi_width = channels - LO
    lines = total // 8
    me = lax.axis_index("lon")
    right, left = lax.rem(me + 1, peers), lax.rem(me + peers - 1, peers)
    sides = (left, right)

    video_copy = pltpu.make_async_copy(video_hbm, video, in_sem.at[0])
    video_copy.start()
    cache_copies = [
        pltpu.make_async_copy(caches_hbm.at[l], caches.at[l], in_sem.at[1 + l]) for l in range(layers)
    ]
    cache_copies[0].start()

    weight_copies = [
        pltpu.make_async_copy(weights_hbm.at[l], raw.at[l], w_sem.at[l]) for l in range(layers)
    ]
    weight_copies[0].start()
    for l in range(1, layers):
        cache_copies[l].start()
        weight_copies[l].start()

    barrier = pltpu.get_barrier_semaphore()

    def greet(k, carry):
        pl.semaphore_signal(
            barrier, inc=1, device_id={"lon": lax.rem(me + k, peers)}, device_id_type=MESH
        )
        return carry

    lax.fori_loop(1, peers, greet, 0)

    params[...] = jnp.zeros_like(params)
    params[0:layers, 0:channels] = gains_ref[...]
    params[8 : 8 + layers, 0:channels] = shifts_ref[...]

    group_row = lax.broadcasted_iota(jnp.int32, (2 * LO, 2 * LO), 0) // (channels // GROUPS)
    group_column = lax.broadcasted_iota(jnp.int32, (2 * LO, 2 * LO), 1) // (channels // GROUPS)
    same_group = jnp.where(group_row == group_column, 1.0, 0.0).astype(BF16)

    lane8 = lax.broadcasted_iota(jnp.int32, (8, LO), 1)

    order = []
    for q in range(3):
        tap = [9 * q + 3 * r for r in range(3)]
        for r in range(3):
            order += [tap[r], tap[r] + 1]
        order += [tap[0] + 2, tap[1] + 2]
        if q != 1:
            order.append(tap[2] + 2)
        if q == 0:
            order.append(9 + 6 + 2)
    unit = LO // 2
    lane_w = lax.broadcasted_iota(jnp.int32, (channels, LO), 1)

    def arrange(l):
        def piece(u, upper):
            tile = raw[l, :, LO * (u // 2) : LO * (u // 2) + LO].astype(F32)
            return tile if u % 2 == upper else pltpu.roll(tile, unit, 1)

        for p in range(3):
            for d in range(0, 26, 2):
                a, b = 27 * p + order[d], 27 * p + order[d + 1]
                if a % 2 == 0 and b == a + 1:
                    weights[l, p, :, unit * d : unit * d + LO] = raw[l, :, unit * a : unit * a + LO]
                else:
                    both = jnp.where(lane_w < unit, piece(a, 0), piece(b, 1))
                    weights[l, p, :, unit * d : unit * d + LO] = both.astype(BF16)
            a = 27 * p + order[26]
            if a % 2 == 0:
                weights[l, p, :, unit * 26 : unit * 27] = raw[l, :, unit * a : unit * a + unit]
            else:
                weights[l, p, :, unit * 26 : unit * 27] = piece(a, 0)[:, 0:unit].astype(BF16)

    def spread(source, target):
        for f in range(frames):
            for hi in range(2):
                size = hi_width if hi else LO
                lanes = pl.ds(LO * hi, size)
                top = source[f, 0:half, :, lanes].astype(F32)
                bottom = source[f, half:height, :, lanes].astype(F32)
                both = jnp.concatenate([top, bottom], axis=1).reshape(rows, size)
                target[pl.ds(hi * total + f * rows, rows), 0:size] = both

    def take_edges(source, target):
        for hi in range(2):
            for side in range(2):
                column = source[pl.ds(hi * total + (width - 1) * side, lines, stride=8), :]
                target[side, hi, 0:lines, :] = column.astype(BF16)

    def edge_copies(source, target, send, recv, l):
        return [
            pltpu.make_async_remote_copy(
                src_ref=source.at[l, side],
                dst_ref=target.at[l, 1 - side],
                send_sem=send.at[l, side],
                recv_sem=recv.at[l, 1 - side],
                device_id={"lon": sides[side]},
                device_id_type=MESH,
            )
            for side in range(2)
        ]

    def local_stats(l):
        parts = []
        for hi in range(2):
            v = x[pl.ds(hi * total, total), :].reshape(lines, 8, LO)
            sums = (jnp.sum(v, axis=0), jnp.sum(v * v, axis=0))
            if hi:
                sums = tuple(jnp.where(lane8 < hi_width, t, 0.0) for t in sums)
            parts.append(sums)
        out = [
            jnp.sum(p, axis=0, keepdims=True)
            for p in (parts[0][0], parts[1][0], parts[0][1], parts[1][1])
        ]
        stat = jnp.concatenate(out + [jnp.zeros((4, LO), F32)], axis=0)
        stat_out[l] = stat
        stat_in[l, peers - 1] = stat

    def send_stats(l):
        def send(k, carry):
            pltpu.make_async_remote_copy(
                src_ref=stat_out.at[l],
                dst_ref=stat_in.at[l, k - 1],
                send_sem=stat_send.at[l],
                recv_sem=stat_recv.at[l],
                device_id={"lon": lax.rem(me + k, peers)},
                device_id_type=MESH,
            ).start()
            return carry

        lax.fori_loop(1, peers, send, 0)

    def stats_wait(sem, l):
        others = stat_in.at[l, pl.ds(0, peers - 1)]
        pltpu.make_async_copy(others, others, sem.at[l]).wait()

    def norm_terms(l):
        sums = jnp.sum(stat_in[l], axis=0)
        wide = jnp.concatenate(
            [
                jnp.concatenate([sums[0:1], sums[1:2]], axis=1),
                jnp.concatenate([sums[2:3], sums[3:4]], axis=1),
                jnp.zeros((6, 2 * LO), F32),
            ],
            axis=0,
        )
        first = wide.astype(BF16)
        rest = wide - first.astype(F32)
        second = rest.astype(BF16)
        third = (rest - second.astype(F32)).astype(BF16)
        grouped = sum(
            jnp.dot(piece, same_group, preferred_element_type=F32)
            for piece in (third, second, first)
        )
        entries = total * peers * (channels // GROUPS)
        average = grouped[0:1] / entries
        variance = jnp.maximum(grouped[1:2] / entries - average * average, 0.0)
        scale = lax.rsqrt(variance + EPSILON) * params[l : l + 1, :] * 0.5
        shift = params[8 + l : 9 + l, :] * 0.5
        return [
            tuple(t[:, LO * hi : LO * hi + LO] for t in (average, scale, shift)) for hi in range(2)
        ]

    def activate(v, terms):
        average, scale, shift = terms
        h = (v - average) * scale + shift
        return h + h * jnp.tanh(h)

    def place_edges(source, target, terms):
        for side in range(2):
            for hi in range(2):
                v = source[side, hi, 0:lines, :].astype(F32)
                if terms is not None:
                    v = activate(v, terms[hi])
                target[side, pl.ds(hi * total + (width - 1) * side, lines, stride=8), :] = v

    steps = 5 if half % 5 == 0 else 1
    size_i = half // steps
    block = size_i * 16
    column = lax.broadcasted_iota(jnp.int32, (2 * size_i, 8, LO), 1)
    lane = lax.broadcasted_iota(jnp.int32, (block, LO), 1)
    lane16 = lax.broadcasted_iota(jnp.int32, (16, LO), 1)

    def swap(v):
        return pltpu.roll(v, LO // 2, 1)

    def build(source, halo, target, terms, store, only):
        for f in only:

            def step(s, following):
                c = steps - 1 - s
                base = f * rows + c * block
                at = pl.ds(16 + c * block, block)
                wide = []
                for hi in range(2):
                    here = pl.ds(hi * total + base, block)
                    v = source[here, :]
                    if terms is not None:
                        v = activate(v, terms[hi])
                    v3 = v.reshape(2 * size_i, 8, LO)
                    before = jnp.where(
                        column == 0,
                        halo[0, here, :].reshape(2 * size_i, 8, LO),
                        pltpu.roll(v3, 1, 1),
                    ).reshape(block, LO)
                    after = jnp.where(
                        column == width - 1,
                        halo[1, here, :].reshape(2 * size_i, 8, LO),
                        pltpu.roll(v3, width - 1, 1),
                    ).reshape(block, LO)
                    wide.append((before, v, after))
                    if store is not None:
                        size = hi_width if hi else LO
                        pair = v.reshape(size_i, 16, LO)
                        for h in range(2):
                            store[
                                f, pl.ds(h * half + c * size_i, size_i), :, LO * hi : LO * hi + size
                            ] = pair[:, 8 * h : 8 * h + 8, 0:size].astype(BF16)
                for r in range(3):
                    target[f, at, LO * r : LO * r + LO] = wide[0][r].astype(BF16)
                before, middle, after = wide[1]
                target[f, at, 384:512] = jnp.where(lane < LO // 2, before, swap(middle)).astype(BF16)
                if block > 16:
                    nexts = jnp.concatenate([after[16:], following], axis=0)
                else:
                    nexts = following
                target[f, at, 512:640] = jnp.where(lane < LO // 2, after, swap(nexts)).astype(BF16)
                return after[0:16]

            following = jnp.zeros((16, LO), F32)
            for s in range(steps):
                following = step(s, following)
            zeros = jnp.zeros((8, 640), F32)
            first = target[f, 16:32, :].astype(F32)
            last = target[f, rows : rows + 16, :].astype(F32)
            over = jnp.concatenate([zeros, last[0:8]], axis=0)
            under = jnp.concatenate([first[8:16], zeros], axis=0)
            target[f, rows + 16 : rows + 32, :] = under.astype(BF16)
            target[f, 0:16, 0:512] = over[:, 0:512].astype(BF16)
            target[f, 0:16, 512:640] = jnp.where(
                lane16 < LO // 2, over[:, 512:640], swap(first[:, 512:640])
            ).astype(BF16)
            target[f, rows : rows + 16, 512:640] = jnp.where(
                lane16 < LO // 2, last[:, 512:640], swap(under[:, 512:640])
            ).astype(BF16)

    def conv(source, f, l, p):
        taps = jnp.concatenate(
            [
                source[f, 0:rows, 0:640],
                source[f, 16 : 16 + rows, 0:512],
                source[f, 32 : 32 + rows, 0:576],
            ],
            axis=1,
        )
        return lax.dot_general(
            taps, weights[l, p], (((1,), (1,)), ((), ())), preferred_element_type=F32
        )

    video_copy.wait()
    spread(video, x)
    local_stats(0)
    take_edges(x, edge_out.at[0])
    pl.semaphore_wait(barrier, peers - 1)
    pending = []
    send_stats(0)
    halo = edge_copies(edge_out, edge_in, edge_send, edge_recv, 0)
    for copy in halo:
        copy.start()

    cache_halos = []

    def send_cache(l):
        cache_copies[l].wait()
        spread(caches.at[l], cx.at[l])
        take_edges(cx.at[l], cedge_out.at[l])
        copies = edge_copies(cedge_out, cedge_in, cedge_send, cedge_recv, l)
        for copy in copies:
            copy.start()
        cache_halos.append(copies)

    def build_cache(l):
        for copy in cache_halos[l]:
            copy.wait()
        place_edges(cedge_in.at[l], chx, None)
        build(cx.at[l], chx, jc, None, None, range(frames))

    for l in range(layers):
        send_cache(l)
    weight_copies[0].wait()
    arrange(0)
    build_cache(0)

    for l in range(layers):
        bias = biases_ref[l : l + 1, :]
        acc[0:rows, :] = conv(jc, 0, l, 0) + bias
        acc[0:rows, :] += conv(jc, 1, l, 1)
        acc[rows:total, :] = conv(jc, 1, l, 0) + bias
        stats_wait(stat_recv, l)
        terms = norm_terms(l)
        for copy in halo:
            copy.wait()
        place_edges(edge_in.at[l], hx, terms)
        if l + 1 < layers:
            for copy in cache_halos[l + 1]:
                copy.wait()
            weight_copies[l + 1].wait()
        build(x, hx, ja, terms, carried.at[l], (0,))
        acc[0:rows, :] += conv(ja, 0, l, 2)
        build(x, hx, ja, terms, carried.at[l], (1,))
        acc[rows:total, :] += conv(ja, 0, l, 1)
        if l + 1 < layers:
            place_edges(cedge_in.at[l + 1], chx, None)
            build(cx.at[l + 1], chx, jc, None, None, range(frames))
            arrange(l + 1)
        acc[rows:total, :] += conv(ja, 1, l, 2)
        out = pltpu.make_async_copy(carried.at[l], carried_hbm.at[l], out_sem.at[l])
        out.start()
        pending.append(out)
        if l == 0:
            for hi in range(2):
                size = hi_width if hi else LO
                x[pl.ds(hi * total, total), 0:size] = acc[:, LO * hi : LO * hi + size]
        elif l == 1:
            spread(video, x)
            for hi in range(2):
                size = hi_width if hi else LO
                x[pl.ds(hi * total, total), 0:size] += acc[:, LO * hi : LO * hi + size]
        else:
            for f in range(frames):
                for hi in range(2):
                    size = hi_width if hi else LO
                    v = (
                        x[pl.ds(hi * total + f * rows, rows), 0:size]
                        + acc[f * rows : f * rows + rows, LO * hi : LO * hi + size]
                    ).reshape(half, 16, size)
                    for h in range(2):
                        encoded[
                            f, h * half : h * half + half, :, LO * hi : LO * hi + size
                        ] = v[:, 8 * h : 8 * h + 8, :].astype(BF16)
        if l + 1 < layers:
            local_stats(l + 1)
            send_stats(l + 1)
            take_edges(x, edge_out.at[l + 1])
            halo = edge_copies(edge_out, edge_in, edge_send, edge_recv, l + 1)
            for copy in halo:
                copy.start()
    out = pltpu.make_async_copy(encoded, encoded_hbm, out_sem.at[layers])
    out.start()
    pending.append(out)
    for l in range(layers):
        stats_wait(stat_send, l)
    for copy in pending:
        copy.wait()


def hand_over(encoded, carried, encoded_out, carried_out, sem):
    layers, frames = carried.shape[:2]
    copies = []
    for f in range(frames):
        copies.append(pltpu.make_async_copy(encoded.at[f], encoded_out.at[f], sem.at[len(copies)]))
        for l in range(layers):
            copies.append(
                pltpu.make_async_copy(carried.at[l, f], carried_out.at[l, f], sem.at[len(copies)])
            )
    for copy in copies:
        copy.start()
    for copy in copies:
        copy.wait()


def local(peers, video_span, caches, norm_gains, shifts, weights, biases):
    frames, height, width, channels = video_span.shape
    layers = caches.shape[0]
    weights = jnp.swapaxes(weights, 1, 2)
    rows = height * 8
    total = frames * rows
    lines = -(-(total // 8) // 16) * 16
    anywhere = pl.BlockSpec(memory_space=pl.ANY)
    vmem = pl.BlockSpec(memory_space=pltpu.VMEM)
    dma = pltpu.SemaphoreType.DMA
    flops = 2 * total * 27 * channels * channels * layers
    encoded, carried = pl.pallas_call(
        functools.partial(kernel, peers),
        out_shape=(
            jax.ShapeDtypeStruct(video_span.shape, BF16),
            jax.ShapeDtypeStruct(caches.shape, BF16),
        ),
        in_specs=[anywhere, anywhere, vmem, vmem, anywhere, vmem],
        out_specs=(anywhere, anywhere),
        scratch_shapes=[
            pltpu.VMEM(video_span.shape, BF16),
            pltpu.VMEM(caches.shape, BF16),
            pltpu.VMEM((layers, channels, 27 * channels), BF16),
            pltpu.VMEM((layers, 3, channels, 9 * channels), BF16),
            pltpu.VMEM((2 * total, LO), F32),
            pltpu.VMEM((layers, 2 * total, LO), F32),
            pltpu.VMEM((total, channels), F32),
            pltpu.VMEM((layers, 2, 2, lines, LO), BF16),
            pltpu.VMEM((layers, 2, 2, lines, LO), BF16),
            pltpu.VMEM((layers, 2, 2, lines, LO), BF16),
            pltpu.VMEM((layers, 2, 2, lines, LO), BF16),
            pltpu.VMEM((2, 2 * total, LO), F32),
            pltpu.VMEM((2, 2 * total, LO), F32),
            pltpu.VMEM((frames, rows + 32, 640), BF16),
            pltpu.VMEM((frames, rows + 32, 640), BF16),
            pltpu.VMEM((layers, 8, LO), F32),
            pltpu.VMEM((layers, peers, 8, LO), F32),
            pltpu.VMEM((16, 2 * LO), F32),
            pltpu.VMEM(caches.shape, BF16),
            pltpu.VMEM(video_span.shape, BF16),
            dma((1 + layers,)),
            dma((layers,)),
            dma((1 + layers,)),
            dma((layers,)),
            dma((layers,)),
            dma((layers, 2)),
            dma((layers, 2)),
            dma((layers, 2)),
            dma((layers, 2)),
        ],
        compiler_params=pltpu.CompilerParams(
            collective_id=0, has_side_effects=True, vmem_limit_bytes=56 * 2**20
        ),
        cost_estimate=pl.CostEstimate(
            flops=flops, bytes_accessed=20 * 2**20, transcendentals=layers * total * channels
        ),
    )(video_span, caches, norm_gains, shifts, weights, biases)
    return pl.pallas_call(
        hand_over,
        out_shape=(
            jax.ShapeDtypeStruct(video_span.shape, BF16),
            jax.ShapeDtypeStruct(caches.shape, BF16),
        ),
        in_specs=[anywhere, anywhere],
        out_specs=(anywhere, anywhere),
        scratch_shapes=[dma(((1 + layers) * frames,))],
    )(encoded, carried)


def solution(mesh):
    return jax.shard_map(
        functools.partial(local, mesh.shape["lon"]),
        mesh=mesh,
        in_specs=(
            P(None, "clips", "lon", None),
            P(None, None, "clips", "lon", None),
            P(),
            P(),
            P(),
            P(),
        ),
        out_specs=(P(None, "clips", "lon", None), P(None, None, "clips", "lon", None)),
        check_vma=False,
    )
```

profile of v0, /device:TPU:0, one launch (start us, length us, event | category | flops | bytes accessed | tf_op | source)
XLA Modules:
  0.0 133.7 jit_solution(16891505631047293821)
XLA Ops:
  0.6 42.4 %shard_map.77 = (bf16[2,90,8,192]{3,2,1,0:T(8,128)(2,1)}, bf16[3,2,90,8,192]{4,3,2,1,0:T(8,128)(2,1)}) custom-call(bf16[2,90,8,192]{3,2,1,0:T(8,128)(2,1)} %video_hbm.1, bf16[3,2,90,8,192]{4,3,2,1,0:T(8,128)(2,1)} %caches_hbm.1, f32[3,192]{1,0:T(4,128)} %gains_ref.1, f32[3,192]{1,0:T(4,128)} %shifts_ref.1, bf16[3,192,5184]{2,1,0:T(8,128)(2,1)} %bitcast.1, ...), custom_call_target="tpu_custom_call" | custom-call | flops 8599633920 | bytes 20971520 | tf_op jit(solution)/shard_map/pallas_call | solution.py:413
  43.0 90.5 %shard_map.78 = (bf16[2,90,8,192]{3,2,1,0:T(8,128)(2,1)}, bf16[3,2,90,8,192]{4,3,2,1,0:T(8,128)(2,1)}) custom-call(bf16[2,90,8,192]{3,2,1,0:T(8,128)(2,1)} %get-tuple-element.4.encoded, bf16[3,2,90,8,192]{4,3,2,1,0:T(8,128)(2,1)} %get-tuple-element.5.carried), custom_call_target="tpu_custom_call" | custom-call | tf_op jit(solution)/shard_map/pallas_call | solution.py:459
where the time goes:
time: 134 us
  Pallas kernels  133 us (99%)
    pallas_call x1, Pallas kernels, local(): pl.pallas_call(hand_over, out_shape=(jax.ShapeDtypeStruct(video_span.shap...  90.5 us
    pallas_call x1, Pallas kernels, local(): pl.pallas_call(functools.partial(kernel, peers), out_shape=(jax.ShapeDtyp...  42.4 us

commit v1 on v0

--- a/solution.py
+++ b/solution.py
@@ -174,14 +174,12 @@
             ],
             axis=0,
         )
-        first = wide.astype(BF16)
-        rest = wide - first.astype(F32)
-        second = rest.astype(BF16)
-        third = (rest - second.astype(F32)).astype(BF16)
-        grouped = sum(
-            jnp.dot(piece, same_group, preferred_element_type=F32)
-            for piece in (third, second, first)
-        )
+        first = wide.astype(BF16).astype(F32)
+        second = (wide - first).astype(BF16).astype(F32)
+        third = wide - first - second
+        pieces = jnp.concatenate([third, second, first], axis=0).astype(BF16)
+        grouped = jnp.dot(pieces, same_group, preferred_element_type=F32)
+        grouped = grouped[0:8] + grouped[8:16] + grouped[16:24]
         entries = total * peers * (channels // GROUPS)
         average = grouped[0:1] / entries
         variance = jnp.maximum(grouped[1:2] / entries - average * average, 0.0)
@@ -274,14 +272,20 @@
                 lane16 < LO // 2, last[:, 512:640], swap(under[:, 512:640])
             ).astype(BF16)
 
-    def conv(source, f, l, p):
+    def conv(source, which, l, p):
         taps = jnp.concatenate(
             [
-                source[f, 0:rows, 0:640],
-                source[f, 16 : 16 + rows, 0:512],
-                source[f, 32 : 32 + rows, 0:576],
+                jnp.concatenate(
+                    [
+                        source[f, 0:rows, 0:640],
+                        source[f, 16 : 16 + rows, 0:512],
+                        source[f, 32 : 32 + rows, 0:576],
+                    ],
+                    axis=1,
+                )
+                for f in which
             ],
-            axis=1,
+            axis=0,
         )
         return lax.dot_general(
             taps, weights[l, p], (((1,), (1,)), ((), ())), preferred_element_type=F32
@@ -298,52 +302,65 @@
     for copy in halo:
         copy.start()
 
-    cache_halos = []
-
-    def send_cache(l):
-        cache_copies[l].wait()
+    cache_halos = [
+        edge_copies(cedge_out, cedge_in, cedge_send, cedge_recv, l) for l in range(layers)
+    ]
+
+    def prepare_cache(l):
         spread(caches.at[l], cx.at[l])
         take_edges(cx.at[l], cedge_out.at[l])
-        copies = edge_copies(cedge_out, cedge_in, cedge_send, cedge_recv, l)
-        for copy in copies:
-            copy.start()
-        cache_halos.append(copies)
 
     def build_cache(l):
-        for copy in cache_halos[l]:
-            copy.wait()
         place_edges(cedge_in.at[l], chx, None)
-        build(cx.at[l], chx, jc, None, None, range(frames))
-
-    for l in range(layers):
-        send_cache(l)
+        build(cx.at[l], chx, jc.at[l % 2], None, None, range(frames))
+
+    cache_copies[0].wait()
+    prepare_cache(0)
+    for copy in cache_halos[0]:
+        copy.start()
     weight_copies[0].wait()
     arrange(0)
+    for copy in cache_halos[0]:
+        copy.wait()
     build_cache(0)
 
     for l in range(layers):
-        bias = biases_ref[l : l + 1, :]
-        acc[0:rows, :] = conv(jc, 0, l, 0) + bias
-        acc[0:rows, :] += conv(jc, 1, l, 1)
-        acc[rows:total, :] = conv(jc, 1, l, 0) + bias
+        if l == 0:
+            for later in range(1, layers):
+                cache_copies[later].wait()
+        elif l + 1 < layers:
+            for copy in cache_halos[l + 1]:
+                copy.wait()
+        if l + 1 < layers:
+            weight_copies[l + 1].wait()
+        now = jc.at[l % 2]
+        acc[...] = conv(now, (0, 1), l, 0) + biases_ref[l : l + 1, :]
+        if l == 0:
+            for later in range(1, layers):
+                prepare_cache(later)
+        elif l + 1 < layers:
+            build_cache(l + 1)
+        if l + 1 < layers:
+            arrange(l + 1)
+        acc[0:rows, :] += conv(now, (1,), l, 1)
+        if l == 0:
+            for later in range(1, layers):
+                for copy in cache_halos[later]:
+                    copy.start()
         stats_wait(stat_recv, l)
         terms = norm_terms(l)
         for copy in halo:
             copy.wait()
         place_edges(edge_in.at[l], hx, terms)
-        if l + 1 < layers:
-            for copy in cache_halos[l + 1]:
+        build(x, hx, ja, terms, carried.at[l], (0,))
+        acc[0:rows, :] += conv(ja, (0,), l, 2)
+        build(x, hx, ja, terms, carried.at[l], (1,))
+        acc[rows:total, :] += conv(ja, (0,), l, 1)
+        if l == 0 and l + 1 < layers:
+            for copy in cache_halos[1]:
                 copy.wait()
-            weight_copies[l + 1].wait()
-        build(x, hx, ja, terms, carried.at[l], (0,))
-        acc[0:rows, :] += conv(ja, 0, l, 2)
-        build(x, hx, ja, terms, carried.at[l], (1,))
-        acc[rows:total, :] += conv(ja, 0, l, 1)
-        if l + 1 < layers:
-            place_edges(cedge_in.at[l + 1], chx, None)
-            build(cx.at[l + 1], chx, jc, None, None, range(frames))
-            arrange(l + 1)
-        acc[rows:total, :] += conv(ja, 1, l, 2)
+            build_cache(1)
+        acc[rows:total, :] += conv(ja, (1,), l, 2)
         out = pltpu.make_async_copy(carried.at[l], carried_hbm.at[l], out_sem.at[l])
         out.start()
         pending.append(out)
@@ -384,18 +401,21 @@
         copy.wait()
 
 
-def hand_over(encoded, carried, encoded_out, carried_out, sem):
+def hand_over(encoded, carried, encoded_out, carried_out, held, held_all, in_sem, out_sem):
     layers, frames = carried.shape[:2]
-    copies = []
+    parts = []
     for f in range(frames):
-        copies.append(pltpu.make_async_copy(encoded.at[f], encoded_out.at[f], sem.at[len(copies)]))
+        parts.append((encoded.at[f], held.at[f], encoded_out.at[f]))
         for l in range(layers):
-            copies.append(
-                pltpu.make_async_copy(carried.at[l, f], carried_out.at[l, f], sem.at[len(copies)])
-            )
-    for copy in copies:
+            parts.append((carried.at[l, f], held_all.at[l, f], carried_out.at[l, f]))
+    ins = [pltpu.make_async_copy(a, b, in_sem.at[i]) for i, (a, b, _) in enumerate(parts)]
+    outs = [pltpu.make_async_copy(b, c, out_sem.at[i]) for i, (_, b, c) in enumerate(parts)]
+    for copy in ins:
         copy.start()
-    for copy in copies:
+    for arrive, leave in zip(ins, outs):
+        arrive.wait()
+        leave.start()
+    for copy in outs:
         copy.wait()
 
 
@@ -432,7 +452,7 @@
             pltpu.VMEM((layers, 2, 2, lines, LO), BF16),
             pltpu.VMEM((2, 2 * total, LO), F32),
             pltpu.VMEM((2, 2 * total, LO), F32),
-            pltpu.VMEM((frames, rows + 32, 640), BF16),
+            pltpu.VMEM((2, frames, rows + 32, 640), BF16),
             pltpu.VMEM((frames, rows + 32, 640), BF16),
             pltpu.VMEM((layers, 8, LO), F32),
             pltpu.VMEM((layers, peers, 8, LO), F32),
@@ -464,7 +484,12 @@
         ),
         in_specs=[anywhere, anywhere],
         out_specs=(anywhere, anywhere),
-        scratch_shapes=[dma(((1 + layers) * frames,))],
+        scratch_shapes=[
+            pltpu.VMEM(video_span.shape, BF16),
+            pltpu.VMEM(caches.shape, BF16),
+            dma(((1 + layers) * frames,)),
+            dma(((1 + layers) * frames,)),
+        ],
     )(encoded, carried)
 
 

time: 134 us -> 47.6 us (0.36)
  Pallas kernels: 133 us -> 46.6 us
    pallas_call x1, Pallas kernels: 90.5 us -> 2.71 us  [local(): pl.pallas_call(hand_over, out_shape=(jax.ShapeDtypeStruct(video_span.shap...]
    pallas_call x1, Pallas kernels: 42.4 us -> 43.9 us  [local(): pl.pallas_call(functools.partial(kernel, peers), out_shape=(jax.ShapeDtyp...]
where the time goes in v1:
time: 47.6 us; the launch traced here: 47.4 us
  Pallas kernels  46.6 us (98%)
  between operations  0.8 us (2%)
    pallas_call x1, Pallas kernels, local(): pl.pallas_call(functools.partial(kernel, peers), out_shape=(jax.ShapeDtyp...  43.9 us
    pallas_call x1, Pallas kernels, local(): pl.pallas_call(hand_over, out_shape=(jax.ShapeDtypeStruct(video_span.shap...  2.71 us

profile of v1, /device:TPU:0, one launch (start us, length us, event | category | flops | bytes accessed | tf_op | source)
XLA Modules:
  0.0 47.4 jit_solution(12444379373731735477)
XLA Ops:
  0.6 43.9 %shard_map.77 = (bf16[2,90,8,192]{3,2,1,0:T(8,128)(2,1)}, bf16[3,2,90,8,192]{4,3,2,1,0:T(8,128)(2,1)}) custom-call(bf16[2,90,8,192]{3,2,1,0:T(8,128)(2,1)} %video_hbm.1, bf16[3,2,90,8,192]{4,3,2,1,0:T(8,128)(2,1)} %caches_hbm.1, f32[3,192]{1,0:T(4,128)} %gains_ref.1, f32[3,192]{1,0:T(4,128)} %shifts_ref.1, bf16[3,192,5184]{2,1,0:T(8,128)(2,1)} %bitcast.1, ...), custom_call_target="tpu_custom_call" | custom-call | flops 8599633920 | bytes 20971520 | tf_op jit(solution)/shard_map/pallas_call | solution.py:433
  44.5 2.7 %shard_map.78 = (bf16[2,90,8,192]{3,2,1,0:T(8,128)(2,1)}, bf16[3,2,90,8,192]{4,3,2,1,0:T(8,128)(2,1)}) custom-call(bf16[2,90,8,192]{3,2,1,0:T(8,128)(2,1)} %get-tuple-element.4.encoded, bf16[3,2,90,8,192]{4,3,2,1,0:T(8,128)(2,1)} %get-tuple-element.5.carried), custom_call_target="tpu_custom_call" | custom-call | tf_op jit(solution)/shard_map/pallas_call | solution.py:479
